TPU v7x, 128 devices: a whole 4x4x4 slice. The times are simulated.
128 devices in a mesh: ctx: 32 (over x, z, core), tp: 4 (over y).
Axes of the slice: x: 4, y: 4, z: 4, core: 2. Of those that a mesh axis runs over, the one named last changes fastest.
Arguments:
- queries: bfloat16 [16384, 4096], P('ctx', 'tp'), may hold values from -160 to 160
- slot_table: int32 [256, 4], P('ctx'), may hold values from -1 to 831, as said below
- states: bfloat16 [832, 128, 512], P('ctx'), may hold values from -6 to 6
- key_weight: bfloat16 [512, 4096], P(None, 'tp'), may hold values from -0.25 to 0.25
- value_weight: bfloat16 [512, 4096], P(None, 'tp'), may hold values from -0.25 to 0.25
- out_grad: bfloat16 [16384, 4096], P('ctx', 'tp'), may hold values from -6 to 6
Outputs:
- attended: bfloat16 [16384, 4096], P('ctx', 'tp')
- query_grad: bfloat16 [16384, 4096], P('ctx', 'tp')
- states_grad: bfloat16 [832, 128, 512], P('ctx', None, 'tp')
- key_weight_grad: float32 [512, 4096], P('ctx', 'tp')
- value_weight_grad: float32 [512, 4096], P('ctx', 'tp')
Inputs may be any that keep to these rules, and one draw needn't show every extreme that they name: `slot_table`: row c of the table lists the slots of stretch c's neighbours: 1 to 4 slot numbers first, then -1; one row in every draw has 4. Every slot appears exactly once. Of the neighbours of one device's 8 stretches, at most 2 are stored in the slots of any one device, and that many in some pair of devices in every draw.
All inputs are finite; a program needn't handle non-finite values.
Results may differ from a plain program's by a relative error of at most 0.023.
The roundings to bfloat16 on the way count: a program that leaves them out, or rounds other values in their place, can miss the bound.
Values may be sent and summed in bfloat16 or wider, within the bound.
No kernel may reach another device: no remote copies, remote signals or barrier semaphores. Data moves between devices by JAX's collectives and lax.ppermute only.
A program may use at most 192 MiB of HBM per device.

v0:
```python
import functools

import jax
import jax.numpy as jnp
from jax import lax
from jax.experimental import pallas as pl
from jax.experimental.pallas import tpu as pltpu
from jax.sharding import PartitionSpec as P

HEAD_DIM = 128
CHUNK = 4
F32 = jnp.float32
BF16 = jnp.bfloat16
NN = (((1,), (0,)), ((), ()))
NT = (((1,), (1,)), ((), ()))
TN = (((0,), (0,)), ((), ()))
MIB = 2**20


def dot(a, b, dims=NN):
    return lax.dot_general(a, b, dims, preferred_element_type=F32)


def attend_kernel(
    counts, quarters, s0, s1, s2, s3, w, wt, q_ref, do_ref, *rest, heads, span, first, before, last
):
    att, qg, p0, p1, p2, p3, out, kv, grads, total = rest[-10:]
    c = pl.program_id(0)
    width = heads * HEAD_DIM
    scale = HEAD_DIM ** (-0.5)
    length = q_ref.shape[0]
    zero = jnp.zeros((length, HEAD_DIM), BF16)
    live = counts[first + c]

    def spread(ref, lo):
        top = jnp.concatenate([ref[:, lo : lo + HEAD_DIM], zero], axis=1)
        low = jnp.concatenate([zero, ref[:, lo + HEAD_DIM : lo + 2 * HEAD_DIM]], axis=1)
        return jnp.concatenate([top, low], axis=0)

    def stretch(met):
        rows = met * span
        states = jnp.concatenate([s[:rows] for s in (s0, s1, s2, s3)], axis=1)
        kv[:rows] = dot(states, w[...]).astype(BF16)
        mask = lax.broadcasted_iota(jnp.int32, (rows, 1), 0) < live * span
        for h in range(0, heads, 2):
            lo = h * HEAD_DIM
            mid, hi = lo + HEAD_DIM, lo + 2 * HEAD_DIM
            q = spread(q_ref, lo)
            do = spread(do_ref, lo)
            k = kv[:rows, lo:hi]
            v = kv[:rows, width + lo : width + hi]
            scores = jnp.where(mask, dot(k, q, NT), -jnp.inf)
            dprobs = dot(v, do, NT)
            expo = jnp.exp((scores - jnp.max(scores, axis=0, keepdims=True)) * scale)
            probs = expo * (1.0 / jnp.sum(expo, axis=0, keepdims=True))
            dscores = probs * (dprobs - jnp.sum(probs * dprobs, axis=0, keepdims=True))
            probs_b = probs.astype(BF16)
            dscores_b = dscores.astype(BF16)
            grads[:rows, width + lo : width + hi] = dot(probs_b, do).astype(BF16)
            grads[:rows, lo:hi] = (dot(dscores_b, q) * scale).astype(BF16)
            both = dot(probs_b, v, TN).astype(BF16)
            att[:, lo:mid] = both[:length, :HEAD_DIM]
            att[:, mid:hi] = both[length:, HEAD_DIM:]
            both = (dot(dscores_b, k, TN) * scale).astype(BF16)
            qg[:, lo:mid] = both[:length, :HEAD_DIM]
            qg[:, mid:hi] = both[length:, HEAD_DIM:]
        terms = dot(states, grads[:rows], TN)
        if before:
            total[...] = jnp.where(c == 0, rest[0][...], total[...]) + terms
        else:

            @pl.when(c == 0)
            def _():
                total[...] = terms

            @pl.when(c > 0)
            def _():
                total[...] += terms

        part = dot(grads[:rows], wt[...]).astype(BF16)
        n = p0.shape[1]
        for r, p in enumerate((p0, p1, p2, p3)):
            p[:rows] = part[:, r * n : (r + 1) * n]

    most = s0.shape[0] // span
    if not before:
        stretch(most)
        cases = ()
    else:
        cases = range(2, most + 1)
    for met in cases:
        here = live <= met if met == 2 else live == met
        pl.when(here)(functools.partial(stretch, met))

    @pl.when(c == pl.num_programs(0) - 1)
    def _():
        if not last:
            out[...] = total[...]
            return
        n = p0.shape[1]
        for r in range(4):
            at = pl.ds(pl.multiple_of(quarters[r] * n, n), n)
            out[at, :] = total[r * n : (r + 1) * n, :].astype(BF16)


def attend(counts, quarters, pieces, w, wt, q, do, terms, after, first, number, span):
    heads = q.shape[1] // HEAD_DIM
    stretches = counts.shape[0]
    length = q.shape[0] // stretches
    width = q.shape[1]
    rows = pieces[0].shape[0] // number
    part = pieces[0].shape[1]
    last = first + number == stretches
    piece = pl.BlockSpec((rows, part), lambda c, *_: (c, 0))
    token = pl.BlockSpec((length, width), lambda c, *_: (first + c, 0))
    token_out = pl.BlockSpec((length, width), lambda c, *_: (c, 0))
    anywhere = pl.BlockSpec(memory_space=pl.ANY)

    def fixed(a):
        return pl.BlockSpec(a.shape, lambda c, *_: (0, 0), pipeline_mode=pl.Buffered(1))

    shape = jax.ShapeDtypeStruct
    sums = shape(w.shape, BF16 if last else F32)
    return pl.pallas_call(
        functools.partial(
            attend_kernel, heads=heads, span=span, first=first, before=bool(terms), last=last
        ),
        grid_spec=pltpu.PrefetchScalarGridSpec(
            num_scalar_prefetch=2,
            grid=(number,),
            in_specs=[piece] * 4
            + [fixed(w), fixed(wt), token, token]
            + [fixed(t) for t in terms]
            + [anywhere] * len(after),
            out_specs=[token_out, token_out] + [piece] * 4 + [fixed(sums)],
            scratch_shapes=[
                pltpu.VMEM((rows, 2 * width), BF16),
                pltpu.VMEM((rows, 2 * width), BF16),
                pltpu.VMEM(w.shape, F32),
            ],
        ),
        out_shape=[shape((number * length, width), BF16)] * 2
        + [shape((number * rows, part), BF16)] * 4
        + [sums],
        compiler_params=pltpu.CompilerParams(vmem_limit_bytes=60 * MIB),
        cost_estimate=pl.CostEstimate(
            flops=number * 6_000_000_000, bytes_accessed=4_000_000, transcendentals=0
        ),
    )(counts, quarters, *pieces, w, wt, q, do, *terms, *after)


def pick_kernel(at, source, out):
    for i in range(out.shape[0]):
        out[i] = source[at[i]]


def pick(at, states, quarter, part):
    slots, span, _ = states.shape
    shape = at.shape + (span, part)
    at = jnp.concatenate([at, quarter.reshape(1)])
    return pl.pallas_call(
        pick_kernel,
        grid_spec=pltpu.PrefetchScalarGridSpec(
            num_scalar_prefetch=1,
            grid=(1,),
            in_specs=[pl.BlockSpec((slots, span, part), lambda i, at: (0, 0, at[shape[0]]))],
            out_specs=pl.BlockSpec(shape, lambda i, at: (0, 0, 0)),
        ),
        out_shape=jax.ShapeDtypeStruct(shape, states.dtype),
        compiler_params=pltpu.CompilerParams(vmem_limit_bytes=60 * MIB),
        cost_estimate=pl.CostEstimate(flops=0, bytes_accessed=4_000_000, transcendentals=0),
    )(at, states)


def merge_kernel(at, earlier, a, b, c, d, out, total):
    half = earlier.shape[0]
    total[:half] = earlier[...]
    whole = a[...].astype(F32) + b[...].astype(F32) + (c[...].astype(F32) + d[...].astype(F32))
    total[half:] = whole.astype(BF16).reshape(earlier.shape)
    for i in range(out.shape[0]):
        out[i] = total[at[i]]


def merge(at, earlier, last):
    half, span, part = earlier.shape
    shape = at.shape + (span, part)
    flat = pl.BlockSpec((half * span, part), lambda i, at: (0, 0))
    return pl.pallas_call(
        merge_kernel,
        grid_spec=pltpu.PrefetchScalarGridSpec(
            num_scalar_prefetch=1,
            grid=(1,),
            in_specs=[pl.BlockSpec(earlier.shape, lambda i, at: (0, 0, 0))] + [flat] * 4,
            out_specs=pl.BlockSpec(shape, lambda i, at: (0, 0, 0)),
            scratch_shapes=[pltpu.VMEM((2 * half, span, part), BF16)],
        ),
        out_shape=jax.ShapeDtypeStruct(shape, BF16),
        compiler_params=pltpu.CompilerParams(vmem_limit_bytes=24 * MIB),
        cost_estimate=pl.CostEstimate(flops=0, bytes_accessed=4_000_000, transcendentals=0),
    )(at, earlier, *last)


def body(queries, slot_table, states, key_weight, value_weight, out_grad):
    devices = lax.axis_size("ctx")
    groups = lax.axis_size("tp")
    me = lax.axis_index("tp")
    stretches, neighbours = slot_table.shape
    slots, span, enc = states.shape
    capacity = 2
    places = devices * capacity
    part = enc // groups
    width = key_weight.shape[1]

    flat = slot_table.reshape(-1)
    live = flat >= 0
    owner = jnp.where(live, flat // slots, -1)
    count = flat.shape[0]
    order = jnp.arange(count)
    alike = (owner[:, None] == owner[None, :]) & (order[None, :] < order[:, None])
    rank = jnp.sum(alike.astype(jnp.int32), axis=1)
    place = jnp.where(live, owner * capacity + rank, -1)
    counts = jnp.sum(live.reshape(stretches, neighbours).astype(jnp.int32), axis=1)
    hit = place[:, None] == jnp.arange(places)[None, :]
    asked = jnp.sum(jnp.where(hit, (flat % slots + 1)[:, None], 0), axis=0) - 1
    source = jnp.sum(jnp.where(hit, order[:, None], 0), axis=0)
    wanted = lax.all_to_all(asked.reshape(devices, capacity), "ctx", 0, 0, tiled=True).reshape(-1)
    goes = wanted[None, :] == jnp.arange(slots)[:, None]
    landing = jnp.sum(jnp.where(goes, jnp.arange(places)[None, :], 0), axis=1)

    quarters = (me + jnp.array([0, groups - 1, 1, 2], jnp.int32)) % groups
    both = jnp.concatenate([key_weight, value_weight], axis=1)
    w = jnp.take(both.reshape(groups, part, 2 * width), quarters, axis=0, mode="clip")
    w = w.reshape(enc, 2 * width)
    wt = w.T

    picked = pick(jnp.maximum(wanted, 0), states, me, part)
    arrived = lax.all_to_all(
        picked.reshape(devices, capacity, span, part), "ctx", 0, 0, tiled=True
    ).reshape(places, span, part)
    opening = jnp.repeat(place.reshape(stretches, neighbours)[:, :1], neighbours, axis=1)
    filled = jnp.where(live, place, opening.reshape(-1))

    def shift(by):
        return [(i, (i + by) % groups) for i in range(groups)]

    def permute(x, by):
        return lax.ppermute(x, "tp", shift(by))

    chunks = stretches // CHUNK
    here = CHUNK * neighbours
    owns = [
        jnp.take(arrived, filled[c * here : (c + 1) * here], axis=0, mode="clip").reshape(
            here * span, part
        )
        for c in range(chunks)
    ]

    def collect(own, after):
        if after:
            own, *_ = lax.optimization_barrier((own, *after))
        return [own, permute(own, 1), permute(own, -1), permute(own, 2)]

    pieces = [collect(owns[0], ())]
    after, terms, got = (), (), ()
    done, summed = [], []
    for c in range(chunks):
        if c < chunks - 1:
            pieces.append(collect(owns[c + 1], pieces[-1][1:]))
        *tokens, p0, p1, p2, p3, sums = attend(
            counts, quarters, pieces[c], w, wt, queries, out_grad, terms, after, c * CHUNK, CHUNK, span
        )
        done.append(tokens)
        terms = (sums,)
        p0, p1, p2, p3, sums, *_ = lax.optimization_barrier(
            (p0, p1, p2, p3, sums, *pieces[-1][1:], *got)
        )
        far = permute(p3, 2)
        if c == chunks - 1:
            core = lax.axis_index("ctx") % 2
            shares = sums.reshape(devices // 2, 2, enc // devices, 2 * width)
            keep = lax.dynamic_index_in_dim(shares, core, 1, keepdims=False)
            send = lax.dynamic_index_in_dim(shares, 1 - core, 1, keepdims=False)
            found = lax.ppermute(send, "ctx", [(i, i ^ 1) for i in range(devices)])
            chip = (keep.astype(F32) + found.astype(F32)).astype(BF16)
            p1, p2, chip, far = lax.optimization_barrier((p1, p2, chip, far))
        got = [p0, permute(p1, -1), permute(p2, 1), far]
        after = summed[-1:]
        if c < chunks - 1:
            total = sum(g.astype(F32) for g in got)
            summed.append(total.astype(BF16).reshape(here, span, part))
    attended, query_grad = (jnp.concatenate([t[i] for t in done], axis=0) for i in range(2))

    same = [list(range(c, devices, 2)) for c in range(2)]
    chip = lax.all_to_all(chip, "ctx", 0, 0, axis_index_groups=same, tiled=True)
    weight_grads = jnp.sum(chip.astype(F32), axis=0)

    leaving = merge(source, jnp.concatenate(summed, axis=0), got)
    landed = lax.all_to_all(
        leaving.reshape(devices, capacity, span, part), "ctx", 0, 0, tiled=True
    ).reshape(places, span, part)
    states_grad = jnp.take(landed, landing, axis=0, mode="clip")
    return (
        attended,
        query_grad,
        states_grad,
        weight_grads[:, :width],
        weight_grads[:, width:],
    )


def solution(mesh):
    in_specs = (
        P("ctx", "tp"),
        P("ctx", None),
        P("ctx", None, None),
        P(None, "tp"),
        P(None, "tp"),
        P("ctx", "tp"),
    )
    out_specs = (
        P("ctx", "tp"),
        P("ctx", "tp"),
        P("ctx", None, "tp"),
        P("ctx", "tp"),
        P("ctx", "tp"),
    )
    return jax.shard_map(body, mesh=mesh, in_specs=in_specs, out_specs=out_specs, check_vma=False)
```

profile of v0, /device:TPU:1, one launch (start us, length us, event | category | flops | bytes accessed | tf_op | source)
XLA Modules:
  0.0 235.8 jit_solution(7044978033697980238)
XLA Ops:
  3.8 9.4 %all-to-all-start = ((s32[32,1,2]{2,1,0:T(1,128)}), s32[32,1,2]{2,1,0:T(1,128)S(1)}, u32[]{:S(2)}, u32[]{:S(2)}) async-start(s32[32,1,2]{2,1,0:T(1,128)} %bitcast), calls=%async_computation | async-start | bytes 32768 | tf_op jit(solution)/shard_map/all_to_all | solution.py:226
  13.2 6.9 %all-to-all-done = s32[32,1,2]{2,1,0:T(1,128)S(1)} async-done(((s32[32,1,2]{2,1,0:T(1,128)}), s32[32,1,2]{2,1,0:T(1,128)S(1)}, u32[]{:S(2)}, u32[]{:S(2)}) %all-to-all-start) | async-done | bytes 288 | tf_op jit(solution)/shard_map/all_to_all | solution.py:226
  22.0 3.3 %shard_map.110 = bf16[64,128,128]{2,1,0:T(8,128)(2,1)} custom-call(s32[65]{0:T(128)} %pad_add_fusion.at, bf16[26,128,512]{2,1,0:T(8,128)(2,1)} %source.1), custom_call_target="tpu_custom_call" | custom-call | bytes 4000000 | tf_op jit(solution)/shard_map/pallas_call | solution.py:161
  25.3 4.4 %all-to-all-start.1 = ((bf16[32,2,128,128]{3,2,1,0:T(8,128)(2,1)}), bf16[32,2,128,128]{3,2,1,0:T(8,128)(2,1)S(1)}, u32[]{:S(2)}, u32[]{:S(2)}) async-start(bf16[32,2,128,128]{3,2,1,0:T(8,128)(2,1)} %bitcast.24), calls=%async_computation.1 | async-start | bytes 4194304 | tf_op jit(solution)/shard_map/all_to_all | solution.py:237
  29.8 28.3 %all-to-all-done.1 = bf16[32,2,128,128]{3,2,1,0:T(8,128)(2,1)S(1)} async-done(((bf16[32,2,128,128]{3,2,1,0:T(8,128)(2,1)}), bf16[32,2,128,128]{3,2,1,0:T(8,128)(2,1)S(1)}, u32[]{:S(2)}, u32[]{:S(2)}) %all-to-all-start.1) | async-done | bytes 2097184 | tf_op jit(solution)/shard_map/all_to_all | solution.py:237
  58.1 1.5 gather_fusion
  59.6 1.3 collective-permute-start
  60.9 1.4 collective-permute-start.1
  62.3 1.6 collective-permute-start.2
  64.0 2.7 %pad_maximum_fusion = bf16[512,2048]{1,0:T(8,128)(2,1)} fusion(bf16[512,1024]{1,0:T(8,128)(2,1)S(1)} %copy-done.4, bf16[512,1024]{1,0:T(8,128)(2,1)} %param.10), kind=kLoop, calls=%fused_computation.4 | loop fusion | flops 4194304 | bytes 4194304 | tf_op jit(solution)/shard_map/concatenate | solution.py:231
  66.7 2.3 gather_fusion.1
  69.0 2.7 %copy.41 = bf16[512,2048]{0,1:T(8,128)(2,1)} copy(bf16[512,2048]{1,0:T(8,128)(2,1)S(1)} %bitcast.21) | data formatting | bytes 4194304 | tf_op jit(solution)/shard_map/reshape | solution.py:233
  71.8 2.2 gather_fusion.2
  74.0 12.1 %collective-permute-done.2.s3 = bf16[2048,128]{1,0:T(8,128)(2,1)} collective-permute-done((bf16[2048,128]{1,0:T(8,128)(2,1)}, bf16[2048,128]{1,0:T(8,128)(2,1)}, u32[]{:S(2)}, u32[]{:S(2)}) %collective-permute-start.2) | collective-permute-done | bytes 524320 | tf_op jit(solution)/shard_map/ppermute | solution.py:247
  86.7 2.1 collective-permute-start.4
  88.9 31.4 %shard_map.111 = (bf16[256,1024]{1,0:T(8,128)(2,1)}, bf16[256,1024]{1,0:T(8,128)(2,1)}, bf16[2048,128]{1,0:T(8,128)(2,1)}, bf16[2048,128]{1,0:T(8,128)(2,1)}, bf...) custom-call(s32[8]{0:T(128)} %get-tuple-element.71.counts, s32[4]{0:T(128)} %copy-done.15, ...), custom_call_target="tpu_custom_call" | custom-call | flops 24000000000 | bytes 4000000 | tf_op jit(solution)/shard_map/pallas_call | solution.py:124
  120.3 1.8 collective-permute-start.6
  122.2 2.7 %collective-permute-start.8 = (bf16[2048,128]{1,0:T(8,128)(2,1)}, bf16[2048,128]{1,0:T(8,128)(2,1)S(1)}, u32[]{:S(2)}, u32[]{:S(2)}) collective-permute-start(bf16[2048,128]{1,0:T(8,128)(2,1)} %get-tuple-element.46), channel_id=1, source_target_pairs={{0,2},{1,3},{2,0},{3,1},{4,6},{5,7},{6,4},{7,5},{8,10},{9,11},{10,... | collective-permute-start | bytes 1572872 | tf_op jit(solution)/shard_map/ppermute | solution.py:247
  124.8 28.7 %shard_map.112 = (bf16[256,1024]{1,0:T(8,128)(2,1)}, bf16[256,1024]{1,0:T(8,128)(2,1)}, bf16[2048,128]{1,0:T(8,128)(2,1)}, bf16[2048,128]{1,0:T(8,128)(2,1)}, bf...) custom-call(s32[8]{0:T(128)} %get-tuple-element.71.counts, s32[4]{0:T(128)} %copy-done.15, ...), custom_call_target="tpu_custom_call" | custom-call | flops 24000000000 | bytes 4000000 | tf_op jit(solution)/shard_map/pallas_call | solution.py:124
  153.7 2.9 %dynamic-slice_bitcast_fusion = bf16[16,16,2048]{2,1,0:T(8,128)(2,1)} fusion(bf16[16,2,16,2048]{3,2,1,0:T(8,128)(2,1)} %bitcast.28, s32[]{:T(128)S(6)} %select_n.104), kind=kLoop, calls=%fused_computation.10 | loop fusion | bytes 2097156 | tf_op jit(solution)/shard_map/jit(dynamic_index_in_dim)/squeeze | solution.py:282
  156.6 2.5 %collective-permute-start.9 = (bf16[16,16,2048]{2,1,0:T(8,128)(2,1)}, bf16[16,16,2048]{2,1,0:T(8,128)(2,1)}, u32[]{:S(2)}, u32[]{:S(2)}) collective-permute-start(bf16[16,16,2048]{2,1,0:T(8,128)(2,1)} %dynamic-slice_bitcast_fusion), channel_id=1, source_target_pairs={{0,4},{4,0},{8,12},{12,8},{16,20},{20,16},{24,28},{28,24},{32,36},... | collective-permute-start | bytes 3145736 | tf_op jit(solution)/shard_map/ppermute | solution.py:283
  159.4 2.3 collective-permute-done.9
  161.7 2.6 %fusion = bf16[16,16,2048]{2,1,0:T(8,128)(2,1)} fusion(bf16[16,16,2048]{2,1,0:T(8,128)(2,1)} %collective-permute-done.9, bf16[16,2,16,2048]{3,2,1,0:T(8,128)(2,1)S(1)} %bitcast.29, s32[]{:T(128)S(6)} %select_n.103), kind=kLoop, calls=%fused_computation.6 | loop fusion | flops 2097152 | bytes 3145732 | tf_op jit(solution)/shard_map/convert_element_type | solution.py:284
  164.3 10.0 %collective-permute-done.10.d = bf16[2048,128]{1,0:T(8,128)(2,1)S(1)} collective-permute-done((bf16[2048,128]{1,0:T(8,128)(2,1)}, bf16[2048,128]{1,0:T(8,128)(2,1)S(1)}, u32[]{:S(2)}, u32[]{:S(2)}) %collective-permute-start.10) | collective-permute-done | bytes 524320 | tf_op jit(solution)/shard_map/ppermute | solution.py:247
  174.3 3.7 %all-to-all-start.3 = ((bf16[16,16,2048]{2,1,0:T(8,128)(2,1)}), bf16[16,16,2048]{2,1,0:T(8,128)(2,1)S(1)}, u32[]{:S(2)}, u32[]{:S(2)}) async-start(bf16[16,16,2048]{2,1,0:T(8,128)(2,1)} %fusion), calls=%async_computation.3 | async-start | bytes 2097152 | tf_op jit(solution)/shard_map/all_to_all | solution.py:294
  179.6 1.5 add_convert_fusion
  181.1 9.5 %collective-permute-done.11.b = bf16[2048,128]{1,0:T(8,128)(2,1)S(1)} collective-permute-done((bf16[2048,128]{1,0:T(8,128)(2,1)}, bf16[2048,128]{1,0:T(8,128)(2,1)S(1)}, u32[]{:S(2)}, u32[]{:S(2)}) %collective-permute-start.11) | collective-permute-done | bytes 524320 | tf_op jit(solution)/shard_map/ppermute | solution.py:247
  190.6 1.7 collective-permute-done.12.c
  192.4 2.5 %shard_map.113 = bf16[64,128,128]{2,1,0:T(8,128)(2,1)} custom-call(s32[64]{0:T(128)S(1)} %get-tuple-element.61.at, bf16[16,128,128]{2,1,0:T(8,128)(2,1)S(1)} %bitcast.20, bf16[2048,128]{1,0:T(8,128)(2,1)S(1)} %copy-done, bf16[2048,128]{1,0:T(8,128)(2,1)S(1)} %collective-permute-done.11.b, bf16[2048,128]{1,0:T(8,128)(2,1)S(1)} %collective-permute-done.12.c, ...), custom_call_target="tpu_custom_call" | custom-call | bytes 4000000 | tf_op jit(solution)/shard_map/pallas_call | solution.py:188
  194.9 9.4 %all-to-all-start.2 = ((bf16[32,2,128,128]{3,2,1,0:T(8,128)(2,1)}), bf16[32,2,128,128]{3,2,1,0:T(8,128)(2,1)}, u32[]{:S(2)}, u32[]{:S(2)}) async-start(bf16[32,2,128,128]{3,2,1,0:T(8,128)(2,1)} %bitcast.13), calls=%async_computation.2 | async-start | bytes 4194304 | tf_op jit(solution)/shard_map/all_to_all | solution.py:298
  207.5 25.1 %all-to-all-done.2 = bf16[32,2,128,128]{3,2,1,0:T(8,128)(2,1)} async-done(((bf16[32,2,128,128]{3,2,1,0:T(8,128)(2,1)}), bf16[32,2,128,128]{3,2,1,0:T(8,128)(2,1)}, u32[]{:S(2)}, u32[]{:S(2)}) %all-to-all-start.2) | async-done | bytes 2097184 | tf_op jit(solution)/shard_map/all_to_all | solution.py:298
  232.7 3.2 %gather_fusion.3 = bf16[26,128,128]{2,1,0:T(8,128)(2,1)} fusion(bf16[64,128,128]{2,1,0:T(8,128)(2,1)} %bitcast.14, s32[1024]{0:T(1024)S(1)} %pad_clamp_fusion), kind=kCustom, calls=%fused_computation.3 | custom fusion | bytes 1704040 | tf_op jit(solution)/shard_map/jit(_take)/gather | solution.py:301
  (88 shorter events, 10.8 us)
Async XLA Ops:
  3.8 16.3 %all-to-all-start = ((s32[32,1,2]{2,1,0:T(1,128)}), s32[32,1,2]{2,1,0:T(1,128)S(1)}, u32[]{:S(2)}, u32[]{:S(2)}) async-start(s32[32,1,2]{2,1,0:T(1,128)} %bitcast), calls=%async_computation | async-start | bytes 32768 | tf_op jit(solution)/shard_map/all_to_all | solution.py:226
  25.3 38.7 %copy-start.19 = (s32[4]{0:T(128)S(1)}, s32[4]{0:T(128)}, u32[]{:S(2)}) copy-start(s32[4]{0:T(128)} %constant.74.clone) | copy-start | bytes 52
  25.3 38.7 %copy-start.4 = (bf16[512,1024]{1,0:T(8,128)(2,1)S(1)}, bf16[512,1024]{1,0:T(8,128)(2,1)}, u32[]{:S(2)}) copy-start(bf16[512,1024]{1,0:T(8,128)(2,1)} %param.11) | copy-start | bytes 3145732
  25.3 32.8 %all-to-all-start.1 = ((bf16[32,2,128,128]{3,2,1,0:T(8,128)(2,1)}), bf16[32,2,128,128]{3,2,1,0:T(8,128)(2,1)S(1)}, u32[]{:S(2)}, u32[]{:S(2)}) async-start(bf16[32,2,128,128]{3,2,1,0:T(8,128)(2,1)} %bitcast.24), calls=%async_computation.1 | async-start | bytes 4194304 | tf_op jit(solution)/shard_map/all_to_all | solution.py:237
  58.1 8.6 %copy-start.2 = (bf16[32,2,128,128]{3,2,1,0:T(8,128)(2,1)}, bf16[32,2,128,128]{3,2,1,0:T(8,128)(2,1)S(1)}, u32[]{:S(2)}) copy-start(bf16[32,2,128,128]{3,2,1,0:T(8,128)(2,1)S(1)} %all-to-all-done.1) | copy-start | bytes 6291460
  59.6 14.4 %collective-permute-start = (bf16[2048,128]{1,0:T(8,128)(2,1)}, bf16[2048,128]{1,0:T(8,128)(2,1)}, u32[]{:S(2)}, u32[]{:S(2)}) collective-permute-start(bf16[2048,128]{1,0:T(8,128)(2,1)} %bitcast.32), channel_id=1, source_target_pairs={{0,1},{1,2},{2,3},{3,0},{4,5},{5,6},{6,7},{7,4},{8,9},{9,10},{10,1... | collective-permute-start | bytes 1572872 | tf_op jit(solution)/shard_map/ppermute | solution.py:247
  60.9 13.1 %collective-permute-start.1 = (bf16[2048,128]{1,0:T(8,128)(2,1)}, bf16[2048,128]{1,0:T(8,128)(2,1)}, u32[]{:S(2)}, u32[]{:S(2)}) collective-permute-start(bf16[2048,128]{1,0:T(8,128)(2,1)} %bitcast.33), channel_id=1, source_target_pairs={{0,3},{1,0},{2,1},{3,2},{4,7},{5,4},{6,5},{7,6},{8,11},{9,8},{10,9... | collective-permute-start | bytes 1572872 | tf_op jit(solution)/shard_map/ppermute | solution.py:247
  62.3 23.8 %collective-permute-start.2 = (bf16[2048,128]{1,0:T(8,128)(2,1)}, bf16[2048,128]{1,0:T(8,128)(2,1)}, u32[]{:S(2)}, u32[]{:S(2)}) collective-permute-start(bf16[2048,128]{1,0:T(8,128)(2,1)} %bitcast.34), channel_id=1, source_target_pairs={{0,2},{1,3},{2,0},{3,1},{4,6},{5,7},{6,4},{7,5},{8,10},{9,11},{10,... | collective-permute-start | bytes 1572872 | tf_op jit(solution)/shard_map/ppermute | solution.py:247
  74.0 46.3 %copy-start.10 = (bf16[16,128,128]{2,1,0:T(8,128)(2,1)}, bf16[16,128,128]{2,1,0:T(8,128)(2,1)S(1)}, u32[]{:S(2)}) copy-start(bf16[16,128,128]{2,1,0:T(8,128)(2,1)S(1)} %gather_fusion.2) | copy-start | bytes 1572868
  86.2 34.1 %collective-permute-start.3 = (bf16[2048,128]{1,0:T(8,128)(2,1)S(1)}, bf16[2048,128]{1,0:T(8,128)(2,1)S(1)}, u32[]{:S(2)}, u32[]{:S(2)}) collective-permute-start(bf16[2048,128]{1,0:T(8,128)(2,1)S(1)} %bitcast.36), channel_id=1, source_target_pairs={{0,1},{1,2},{2,3},{3,0},{4,5},{5,6},{6,7},{7,4},{8,9},{9,10},{10,1... | collective-permute-start | bytes 1572872 | tf_op jit(solution)/shard_map/ppermute | solution.py:247
  86.7 33.6 %collective-permute-start.4 = (bf16[2048,128]{1,0:T(8,128)(2,1)S(1)}, bf16[2048,128]{1,0:T(8,128)(2,1)S(1)}, u32[]{:S(2)}, u32[]{:S(2)}) collective-permute-start(bf16[2048,128]{1,0:T(8,128)(2,1)S(1)} %bitcast.37), channel_id=1, source_target_pairs={{0,3},{1,0},{2,1},{3,2},{4,7},{5,4},{6,5},{7,6},{8,11},{9,8},{10,9... | collective-permute-start | bytes 1572872 | tf_op jit(solution)/shard_map/ppermute | solution.py:247
  88.8 31.5 %collective-permute-start.5 = (bf16[2048,128]{1,0:T(8,128)(2,1)S(1)}, bf16[2048,128]{1,0:T(8,128)(2,1)S(1)}, u32[]{:S(2)}, u32[]{:S(2)}) collective-permute-start(bf16[2048,128]{1,0:T(8,128)(2,1)S(1)} %bitcast.38), channel_id=1, source_target_pairs={{0,2},{1,3},{2,0},{3,1},{4,6},{5,7},{6,4},{7,5},{8,10},{9,11},{10,... | collective-permute-start | bytes 1572872 | tf_op jit(solution)/shard_map/ppermute | solution.py:247
  120.3 4.6 %copy-start.16 = (bf16[2048,128]{1,0:T(8,128)(2,1)}, bf16[2048,128]{1,0:T(8,128)(2,1)S(1)}, u32[]{:S(2)}) copy-start(bf16[2048,128]{1,0:T(8,128)(2,1)S(1)} %collective-permute-done.3.s1) | copy-start | bytes 1572868
  120.3 4.5 %copy-start.17 = (bf16[2048,128]{1,0:T(8,128)(2,1)}, bf16[2048,128]{1,0:T(8,128)(2,1)S(1)}, u32[]{:S(2)}) copy-start(bf16[2048,128]{1,0:T(8,128)(2,1)S(1)} %collective-permute-done.4.s2) | copy-start | bytes 1572868
  120.3 4.5 %copy-start.18 = (bf16[2048,128]{1,0:T(8,128)(2,1)}, bf16[2048,128]{1,0:T(8,128)(2,1)S(1)}, u32[]{:S(2)}) copy-start(bf16[2048,128]{1,0:T(8,128)(2,1)S(1)} %collective-permute-done.5.s3) | copy-start | bytes 1572868
  120.3 33.3 %collective-permute-start.6 = (bf16[2048,128]{1,0:T(8,128)(2,1)}, bf16[2048,128]{1,0:T(8,128)(2,1)S(1)}, u32[]{:S(2)}, u32[]{:S(2)}) collective-permute-start(bf16[2048,128]{1,0:T(8,128)(2,1)} %get-tuple-element.44), channel_id=1, source_target_pairs={{0,3},{1,0},{2,1},{3,2},{4,7},{5,4},{6,5},{7,6},{8,11},{9,8},{10,9... | collective-permute-start | bytes 1572872 | tf_op jit(solution)/shard_map/ppermute | solution.py:247
  122.1 31.5 %collective-permute-start.7 = (bf16[2048,128]{1,0:T(8,128)(2,1)}, bf16[2048,128]{1,0:T(8,128)(2,1)S(1)}, u32[]{:S(2)}, u32[]{:S(2)}) collective-permute-start(bf16[2048,128]{1,0:T(8,128)(2,1)} %get-tuple-element.45), channel_id=1, source_target_pairs={{0,1},{1,2},{2,3},{3,0},{4,5},{5,6},{6,7},{7,4},{8,9},{9,10},{10,1... | collective-permute-start | bytes 1572872 | tf_op jit(solution)/shard_map/ppermute | solution.py:247
  122.2 31.5 %collective-permute-start.8 = (bf16[2048,128]{1,0:T(8,128)(2,1)}, bf16[2048,128]{1,0:T(8,128)(2,1)S(1)}, u32[]{:S(2)}, u32[]{:S(2)}) collective-permute-start(bf16[2048,128]{1,0:T(8,128)(2,1)} %get-tuple-element.46), channel_id=1, source_target_pairs={{0,2},{1,3},{2,0},{3,1},{4,6},{5,7},{6,4},{7,5},{8,10},{9,11},{10,... | collective-permute-start | bytes 1572872 | tf_op jit(solution)/shard_map/ppermute | solution.py:247
  153.6 8.2 %copy-start.3 = (bf16[512,2048]{1,0:T(8,128)(2,1)S(1)}, bf16[512,2048]{1,0:T(8,128)(2,1)}, u32[]{:S(2)}) copy-start(bf16[512,2048]{1,0:T(8,128)(2,1)} %get-tuple-element.55) | copy-start | bytes 6291460
  153.6 5.5 %copy-start.7 = (bf16[2048,128]{1,0:T(8,128)(2,1)}, bf16[2048,128]{1,0:T(8,128)(2,1)S(1)}, u32[]{:S(2)}) copy-start(bf16[2048,128]{1,0:T(8,128)(2,1)S(1)} %collective-permute-done.7) | copy-start | bytes 1572868
  153.6 5.8 %copy-start.8 = (bf16[2048,128]{1,0:T(8,128)(2,1)}, bf16[2048,128]{1,0:T(8,128)(2,1)S(1)}, u32[]{:S(2)}) copy-start(bf16[2048,128]{1,0:T(8,128)(2,1)S(1)} %collective-permute-done.8) | copy-start | bytes 1572868
  156.6 5.2 %collective-permute-start.9 = (bf16[16,16,2048]{2,1,0:T(8,128)(2,1)}, bf16[16,16,2048]{2,1,0:T(8,128)(2,1)}, u32[]{:S(2)}, u32[]{:S(2)}) collective-permute-start(bf16[16,16,2048]{2,1,0:T(8,128)(2,1)} %dynamic-slice_bitcast_fusion), channel_id=1, source_target_pairs={{0,4},{4,0},{8,12},{12,8},{16,20},{20,16},{24,28},{28,24},{32,36},... | collective-permute-start | bytes 3145736 | tf_op jit(solution)/shard_map/ppermute | solution.py:283
  159.1 15.2 %collective-permute-start.10 = (bf16[2048,128]{1,0:T(8,128)(2,1)}, bf16[2048,128]{1,0:T(8,128)(2,1)S(1)}, u32[]{:S(2)}, u32[]{:S(2)}) collective-permute-start(bf16[2048,128]{1,0:T(8,128)(2,1)} %get-tuple-element.56), channel_id=1, source_target_pairs={{0,2},{1,3},{2,0},{3,1},{4,6},{5,7},{6,4},{7,5},{8,10},{9,11},{10,... | collective-permute-start | bytes 1572872 | tf_op jit(solution)/shard_map/ppermute | solution.py:247
  159.4 20.2 %copy-start.5 = (bf16[2048,128]{1,0:T(8,128)(2,1)S(1)}, bf16[2048,128]{1,0:T(8,128)(2,1)}, u32[]{:S(2)}) copy-start(bf16[2048,128]{1,0:T(8,128)(2,1)} %get-tuple-element.43) | copy-start | bytes 1572868
  164.3 15.3 %copy-start.9 = (bf16[2048,128]{1,0:T(8,128)(2,1)S(1)}, bf16[2048,128]{1,0:T(8,128)(2,1)}, u32[]{:S(2)}) copy-start(bf16[2048,128]{1,0:T(8,128)(2,1)} %copy-done.8) | copy-start | bytes 1572868
  164.3 28.0 %copy-start = (bf16[2048,128]{1,0:T(8,128)(2,1)S(1)}, bf16[2048,128]{1,0:T(8,128)(2,1)}, u32[]{:S(2)}) copy-start(bf16[2048,128]{1,0:T(8,128)(2,1)} %get-tuple-element.52.a) | copy-start | bytes 1572868
  174.3 20.6 %all-to-all-start.3 = ((bf16[16,16,2048]{2,1,0:T(8,128)(2,1)}), bf16[16,16,2048]{2,1,0:T(8,128)(2,1)S(1)}, u32[]{:S(2)}, u32[]{:S(2)}) async-start(bf16[16,16,2048]{2,1,0:T(8,128)(2,1)} %fusion), calls=%async_computation.3 | async-start | bytes 2097152 | tf_op jit(solution)/shard_map/all_to_all | solution.py:294
  178.1 12.6 %collective-permute-start.11 = (bf16[2048,128]{1,0:T(8,128)(2,1)}, bf16[2048,128]{1,0:T(8,128)(2,1)S(1)}, u32[]{:S(2)}, u32[]{:S(2)}) collective-permute-start(bf16[2048,128]{1,0:T(8,128)(2,1)} %get-tuple-element.57), channel_id=1, source_target_pairs={{0,3},{1,0},{2,1},{3,2},{4,7},{5,4},{6,5},{7,6},{8,11},{9,8},{10,9... | collective-permute-start | bytes 1572872 | tf_op jit(solution)/shard_map/ppermute | solution.py:247
  178.9 13.4 %collective-permute-start.12 = (bf16[2048,128]{1,0:T(8,128)(2,1)}, bf16[2048,128]{1,0:T(8,128)(2,1)S(1)}, u32[]{:S(2)}, u32[]{:S(2)}) collective-permute-start(bf16[2048,128]{1,0:T(8,128)(2,1)} %get-tuple-element.58), channel_id=1, source_target_pairs={{0,1},{1,2},{2,3},{3,0},{4,5},{5,6},{6,7},{7,4},{8,9},{9,10},{10,1... | collective-permute-start | bytes 1572872 | tf_op jit(solution)/shard_map/ppermute | solution.py:247
  194.9 9.6 %copy-start.12 = (bf16[256,1024]{1,0:T(8,128)(2,1)S(1)}, bf16[256,1024]{1,0:T(8,128)(2,1)}, u32[]{:S(2)}) copy-start(bf16[256,1024]{1,0:T(8,128)(2,1)} %get-tuple-element.37) | copy-start | bytes 1572868
  194.9 9.6 %copy-start.14 = (bf16[256,1024]{1,0:T(8,128)(2,1)S(1)}, bf16[256,1024]{1,0:T(8,128)(2,1)}, u32[]{:S(2)}) copy-start(bf16[256,1024]{1,0:T(8,128)(2,1)} %get-tuple-element.38) | copy-start | bytes 1572868
  194.9 37.8 %all-to-all-start.2 = ((bf16[32,2,128,128]{3,2,1,0:T(8,128)(2,1)}), bf16[32,2,128,128]{3,2,1,0:T(8,128)(2,1)}, u32[]{:S(2)}, u32[]{:S(2)}) async-start(bf16[32,2,128,128]{3,2,1,0:T(8,128)(2,1)} %bitcast.13), calls=%async_computation.2 | async-start | bytes 4194304 | tf_op jit(solution)/shard_map/all_to_all | solution.py:298
  (5 other events, 11.0 us)
where the time goes:
time: 237 us; the launch traced here: 236 us
  waiting for transfers between devices  96 us (41%)
  Pallas kernels  65.9 us (28%)
  starting transfers between devices  43 us (18%)
  local copies, waits for them, and re-layouts  18.5 us (8%)
  other arithmetic  11.4 us (5%)
    pallas_call x2, Pallas kernels, attend(): pl.pallas_call(functools.partial(attend_kernel, heads=heads, span=span, f...  60.1 us
    ppermute x12, waiting for transfers between devices, permute(): return lax.ppermute(x, 'tp', shift(by))  33.4 us
    all_to_all x1, waiting for transfers between devices, body(): lax.all_to_all(picked.reshape(devices, capacity, span, part), 'ctx', 0, 0...  28.3 us
    all_to_all x1, waiting for transfers between devices, body(): lax.all_to_all(leaving.reshape(devices, capacity, span, part), 'ctx', 0,...  25.1 us
    ppermute x12, starting transfers between devices, permute(): return lax.ppermute(x, 'tp', shift(by))  13.4 us
    all_to_all x1, starting transfers between devices, body(): lax.all_to_all(asked.reshape(devices, capacity), 'ctx', 0, 0, tiled=True)  9.43 us
    all_to_all x1, starting transfers between devices, body(): lax.all_to_all(leaving.reshape(devices, capacity, span, part), 'ctx', 0,...  9.42 us
    all_to_all x1, waiting for transfers between devices, body(): lax.all_to_all(asked.reshape(devices, capacity), 'ctx', 0, 0, tiled=True)  6.86 us
  transfers between devices with their start and end apart: 17, of which 8 were waited for; matrix products, arithmetic and copies ran while one was open for 7% of the time, Pallas kernels for 27%

commit v1 on v0

--- a/solution.py
+++ b/solution.py
@@ -22,7 +22,7 @@
 
 
 def attend_kernel(
-    counts, quarters, s0, s1, s2, s3, w, wt, q_ref, do_ref, *rest, heads, span, first, before, last
+    counts, quarters, s0, s1, s2, s3, w, q_ref, do_ref, *rest, heads, span, first, before, last
 ):
     att, qg, p0, p1, p2, p3, out, kv, grads, total = rest[-10:]
     c = pl.program_id(0)
@@ -77,7 +77,7 @@
             def _():
                 total[...] += terms
 
-        part = dot(grads[:rows], wt[...]).astype(BF16)
+        part = dot(grads[:rows], w[...], NT).astype(BF16)
         n = p0.shape[1]
         for r, p in enumerate((p0, p1, p2, p3)):
             p[:rows] = part[:, r * n : (r + 1) * n]
@@ -103,7 +103,7 @@
             out[at, :] = total[r * n : (r + 1) * n, :].astype(BF16)
 
 
-def attend(counts, quarters, pieces, w, wt, q, do, terms, after, first, number, span):
+def attend(counts, quarters, pieces, w, q, do, terms, after, first, number, span):
     heads = q.shape[1] // HEAD_DIM
     stretches = counts.shape[0]
     length = q.shape[0] // stretches
@@ -129,7 +129,7 @@
             num_scalar_prefetch=2,
             grid=(number,),
             in_specs=[piece] * 4
-            + [fixed(w), fixed(wt), token, token]
+            + [fixed(w), token, token]
             + [fixed(t) for t in terms]
             + [anywhere] * len(after),
             out_specs=[token_out, token_out] + [piece] * 4 + [fixed(sums)],
@@ -146,7 +146,7 @@
         cost_estimate=pl.CostEstimate(
             flops=number * 6_000_000_000, bytes_accessed=4_000_000, transcendentals=0
         ),
-    )(counts, quarters, *pieces, w, wt, q, do, *terms, *after)
+    )(counts, quarters, *pieces, w, q, do, *terms, *after)
 
 
 def pick_kernel(at, source, out):
@@ -231,7 +231,6 @@
     both = jnp.concatenate([key_weight, value_weight], axis=1)
     w = jnp.take(both.reshape(groups, part, 2 * width), quarters, axis=0, mode="clip")
     w = w.reshape(enc, 2 * width)
-    wt = w.T
 
     picked = pick(jnp.maximum(wanted, 0), states, me, part)
     arrived = lax.all_to_all(
@@ -267,7 +266,7 @@
         if c < chunks - 1:
             pieces.append(collect(owns[c + 1], pieces[-1][1:]))
         *tokens, p0, p1, p2, p3, sums = attend(
-            counts, quarters, pieces[c], w, wt, queries, out_grad, terms, after, c * CHUNK, CHUNK, span
+            counts, quarters, pieces[c], w, queries, out_grad, terms, after, c * CHUNK, CHUNK, span
         )
         done.append(tokens)
         terms = (sums,)
@@ -282,7 +281,6 @@
             send = lax.dynamic_index_in_dim(shares, 1 - core, 1, keepdims=False)
             found = lax.ppermute(send, "ctx", [(i, i ^ 1) for i in range(devices)])
             chip = (keep.astype(F32) + found.astype(F32)).astype(BF16)
-            p1, p2, chip, far = lax.optimization_barrier((p1, p2, chip, far))
         got = [p0, permute(p1, -1), permute(p2, 1), far]
         after = summed[-1:]
         if c < chunks - 1:

time: 237 us -> 236 us (level)
  Pallas kernels: 65.9 us -> 60.7 us
  starting transfers between devices: 43 us -> 48 us
  waiting for transfers between devices: 96 us -> 101 us
  local copies, waits for them, and re-layouts: 18.5 us -> 14.9 us
    pallas_call x2, Pallas kernels: 60.1 us -> 54.9 us  [attend(): pl.pallas_call(functools.partial(attend_kernel, heads=heads, span=span, f...]
    ppermute x12, waiting for transfers between devices: 33.4 us -> 37.9 us  [permute(): return lax.ppermute(x, 'tp', shift(by))]
    ppermute x1, starting transfers between devices: 2.52 us -> 6.63 us  [body(): found = lax.ppermute(send, 'ctx', [(i, i ^ 1) for i in range(devices)])]
    reshape x1 -> x0, local copies, waits for them, and re-layouts: 2.72 us -> none  [body(): w = w.reshape(enc, 2 * width)]
  transfers between devices with their start and end apart: 17 -> 17, of which waited for: 8 -> 9; matrix products, arithmetic and copies ran while one was open for 7% -> 4% of each run, Pallas kernels for 27% -> 24%
where the time goes in v1:
time: 236 us; the launch traced here: 235 us
  waiting for transfers between devices  101 us (43%)
  Pallas kernels  60.7 us (26%)
  starting transfers between devices  48 us (20%)
  local copies, waits for them, and re-layouts  14.9 us (6%)
  other arithmetic  10 us (4%)
    pallas_call x2, Pallas kernels, attend(): pl.pallas_call(functools.partial(attend_kernel, heads=heads, span=span, f...  54.9 us
    ppermute x12, waiting for transfers between devices, permute(): return lax.ppermute(x, 'tp', shift(by))  37.9 us
    all_to_all x1, waiting for transfers between devices, body(): lax.all_to_all(picked.reshape(devices, capacity, span, part), 'ctx', 0, 0...  28.3 us
    all_to_all x1, waiting for transfers between devices, body(): lax.all_to_all(leaving.reshape(devices, capacity, span, part), 'ctx', 0,...  25.1 us
    ppermute x12, starting transfers between devices, permute(): return lax.ppermute(x, 'tp', shift(by))  15 us
    all_to_all x1, starting transfers between devices, body(): lax.all_to_all(asked.reshape(devices, capacity), 'ctx', 0, 0, tiled=True)  9.43 us
    all_to_all x1, starting transfers between devices, body(): lax.all_to_all(leaving.reshape(devices, capacity, span, part), 'ctx', 0,...  8.56 us
    all_to_all x1, waiting for transfers between devices, body(): lax.all_to_all(asked.reshape(devices, capacity), 'ctx', 0, 0, tiled=True)  6.86 us
  transfers between devices with their start and end apart: 17, of which 9 were waited for; matrix products, arithmetic and copies ran while one was open for 4% of the time, Pallas kernels for 24%

profile of v1, /device:TPU:1, one launch (start us, length us, event | category | flops | bytes accessed | tf_op | source)
XLA Modules:
  0.0 235.3 jit_solution(1086876237459990084)
XLA Ops:
  3.8 9.4 %all-to-all-start = ((s32[32,1,2]{2,1,0:T(1,128)}), s32[32,1,2]{2,1,0:T(1,128)S(1)}, u32[]{:S(2)}, u32[]{:S(2)}) async-start(s32[32,1,2]{2,1,0:T(1,128)} %bitcast), calls=%async_computation | async-start | bytes 32768 | tf_op jit(solution)/shard_map/all_to_all | solution.py:226
  13.2 6.9 %all-to-all-done = s32[32,1,2]{2,1,0:T(1,128)S(1)} async-done(((s32[32,1,2]{2,1,0:T(1,128)}), s32[32,1,2]{2,1,0:T(1,128)S(1)}, u32[]{:S(2)}, u32[]{:S(2)}) %all-to-all-start) | async-done | bytes 288 | tf_op jit(solution)/shard_map/all_to_all | solution.py:226
  22.0 3.3 %shard_map.110 = bf16[64,128,128]{2,1,0:T(8,128)(2,1)} custom-call(s32[65]{0:T(128)} %pad_add_fusion.at, bf16[26,128,512]{2,1,0:T(8,128)(2,1)} %source.1), custom_call_target="tpu_custom_call" | custom-call | bytes 4000000 | tf_op jit(solution)/shard_map/pallas_call | solution.py:161
  25.3 4.4 %all-to-all-start.1 = ((bf16[32,2,128,128]{3,2,1,0:T(8,128)(2,1)}), bf16[32,2,128,128]{3,2,1,0:T(8,128)(2,1)S(1)}, u32[]{:S(2)}, u32[]{:S(2)}) async-start(bf16[32,2,128,128]{3,2,1,0:T(8,128)(2,1)} %bitcast.20), calls=%async_computation.1 | async-start | bytes 4194304 | tf_op jit(solution)/shard_map/all_to_all | solution.py:236
  29.8 28.3 %all-to-all-done.1 = bf16[32,2,128,128]{3,2,1,0:T(8,128)(2,1)S(1)} async-done(((bf16[32,2,128,128]{3,2,1,0:T(8,128)(2,1)}), bf16[32,2,128,128]{3,2,1,0:T(8,128)(2,1)S(1)}, u32[]{:S(2)}, u32[]{:S(2)}) %all-to-all-start.1) | async-done | bytes 2097184 | tf_op jit(solution)/shard_map/all_to_all | solution.py:236
  58.1 1.5 gather_fusion
  60.9 1.4 collective-permute-start.1
  62.3 1.6 collective-permute-start.2
  64.0 1.4 pad_maximum_fusion
  65.5 2.0 gather_fusion.1
  67.5 2.2 gather_fusion.2
  69.8 4.1 %collective-permute-done.s1 = bf16[2048,128]{1,0:T(8,128)(2,1)} collective-permute-done((bf16[2048,128]{1,0:T(8,128)(2,1)}, bf16[2048,128]{1,0:T(8,128)(2,1)}, u32[]{:S(2)}, u32[]{:S(2)}) %collective-permute-start) | collective-permute-done | bytes 524320 | tf_op jit(solution)/shard_map/ppermute | solution.py:246
  73.8 12.3 %collective-permute-done.2.s3 = bf16[2048,128]{1,0:T(8,128)(2,1)} collective-permute-done((bf16[2048,128]{1,0:T(8,128)(2,1)}, bf16[2048,128]{1,0:T(8,128)(2,1)}, u32[]{:S(2)}, u32[]{:S(2)}) %collective-permute-start.2) | collective-permute-done | bytes 524320 | tf_op jit(solution)/shard_map/ppermute | solution.py:246
  86.7 2.1 collective-permute-start.4
  88.9 31.0 %shard_map.111 = (bf16[256,1024]{1,0:T(8,128)(2,1)}, bf16[256,1024]{1,0:T(8,128)(2,1)}, bf16[2048,128]{1,0:T(8,128)(2,1)}, bf16[2048,128]{1,0:T(8,128)(2,1)}, bf...) custom-call(s32[8]{0:T(128)} %get-tuple-element.63.counts, s32[4]{0:T(128)} %copy-done.14, ...), custom_call_target="tpu_custom_call" | custom-call | flops 24000000000 | bytes 4000000 | tf_op jit(solution)/shard_map/pallas_call | solution.py:124
  119.9 1.8 collective-permute-start.6
  121.7 2.7 %collective-permute-start.8 = (bf16[2048,128]{1,0:T(8,128)(2,1)}, bf16[2048,128]{1,0:T(8,128)(2,1)}, u32[]{:S(2)}, u32[]{:S(2)}) collective-permute-start(bf16[2048,128]{1,0:T(8,128)(2,1)} %get-tuple-element.42), channel_id=1, source_target_pairs={{0,2},{1,3},{2,0},{3,1},{4,6},{5,7},{6,4},{7,5},{8,10},{9,11},{10,... | collective-permute-start | bytes 1572872 | tf_op jit(solution)/shard_map/ppermute | solution.py:246
  124.4 24.0 %shard_map.112 = (bf16[256,1024]{1,0:T(8,128)(2,1)}, bf16[256,1024]{1,0:T(8,128)(2,1)}, bf16[2048,128]{1,0:T(8,128)(2,1)}, bf16[2048,128]{1,0:T(8,128)(2,1)}, bf...) custom-call(s32[8]{0:T(128)} %get-tuple-element.63.counts, s32[4]{0:T(128)} %copy-done.14, ...), custom_call_target="tpu_custom_call" | custom-call | flops 24000000000 | bytes 4000000 | tf_op jit(solution)/shard_map/pallas_call | solution.py:124
  149.4 1.3 dynamic-slice_bitcast_fusion
  150.7 6.6 %collective-permute-start.12 = (bf16[16,16,2048]{2,1,0:T(8,128)(2,1)S(1)}, bf16[16,16,2048]{2,1,0:T(8,128)(2,1)}, u32[]{:S(2)}, u32[]{:S(2)}) collective-permute-start(bf16[16,16,2048]{2,1,0:T(8,128)(2,1)S(1)} %dynamic-slice_bitcast_fusion), channel_id=1, source_target_pairs={{0,4},{4,0},{8,12},{12,8},{16,20},{20,16},{24,28},{28,24},{32,36},... | collective-permute-start | bytes 3145736 | tf_op jit(solution)/shard_map/ppermute | solution.py:282
  157.3 2.4 %collective-permute-done.12 = bf16[16,16,2048]{2,1,0:T(8,128)(2,1)} collective-permute-done((bf16[16,16,2048]{2,1,0:T(8,128)(2,1)S(1)}, bf16[16,16,2048]{2,1,0:T(8,128)(2,1)}, u32[]{:S(2)}, u32[]{:S(2)}) %collective-permute-start.12) | collective-permute-done | bytes 1048608 | tf_op jit(solution)/shard_map/ppermute | solution.py:282
  159.7 2.7 %fusion = bf16[16,16,2048]{2,1,0:T(8,128)(2,1)} fusion(bf16[16,16,2048]{2,1,0:T(8,128)(2,1)} %collective-permute-done.12, bf16[16,2,16,2048]{3,2,1,0:T(8,128)(2,1)S(1)} %bitcast.25, s32[]{:T(128)S(6)} %select_n.104), kind=kLoop, calls=%fused_computation.6 | loop fusion | flops 2097152 | bytes 3145732 | tf_op jit(solution)/shard_map/convert_element_type | solution.py:283
  162.4 4.0 %all-to-all-start.3 = ((bf16[16,16,2048]{2,1,0:T(8,128)(2,1)}), bf16[16,16,2048]{2,1,0:T(8,128)(2,1)S(1)}, u32[]{:S(2)}, u32[]{:S(2)}) async-start(bf16[16,16,2048]{2,1,0:T(8,128)(2,1)} %fusion), calls=%async_computation.3 | async-start | bytes 2097152 | tf_op jit(solution)/shard_map/all_to_all | solution.py:292
  168.1 1.8 collective-permute-start.9
  169.9 1.3 add_convert_fusion
  171.2 10.6 %collective-permute-done.10.c = bf16[2048,128]{1,0:T(8,128)(2,1)S(1)} collective-permute-done((bf16[2048,128]{1,0:T(8,128)(2,1)}, bf16[2048,128]{1,0:T(8,128)(2,1)S(1)}, u32[]{:S(2)}, u32[]{:S(2)}) %collective-permute-start.10) | collective-permute-done | bytes 524320 | tf_op jit(solution)/shard_map/ppermute | solution.py:246
  181.8 9.1 %collective-permute-done.11.d = bf16[2048,128]{1,0:T(8,128)(2,1)S(1)} collective-permute-done((bf16[2048,128]{1,0:T(8,128)(2,1)}, bf16[2048,128]{1,0:T(8,128)(2,1)S(1)}, u32[]{:S(2)}, u32[]{:S(2)}) %collective-permute-start.11) | collective-permute-done | bytes 524320 | tf_op jit(solution)/shard_map/ppermute | solution.py:246
  190.9 1.7 collective-permute-done.9.b
  192.7 2.5 %shard_map.113 = bf16[64,128,128]{2,1,0:T(8,128)(2,1)} custom-call(s32[64]{0:T(128)S(1)} %get-tuple-element.53.at, bf16[16,128,128]{2,1,0:T(8,128)(2,1)S(1)} %bitcast.19, bf16[2048,128]{1,0:T(8,128)(2,1)S(1)} %copy-done, bf16[2048,128]{1,0:T(8,128)(2,1)S(1)} %collective-permute-done.9.b, bf16[2048,128]{1,0:T(8,128)(2,1)S(1)} %collective-permute-done.10.c, ...), custom_call_target="tpu_custom_call" | custom-call | bytes 4000000 | tf_op jit(solution)/shard_map/pallas_call | solution.py:188
  195.2 8.6 %all-to-all-start.2 = ((bf16[32,2,128,128]{3,2,1,0:T(8,128)(2,1)}), bf16[32,2,128,128]{3,2,1,0:T(8,128)(2,1)}, u32[]{:S(2)}, u32[]{:S(2)}) async-start(bf16[32,2,128,128]{3,2,1,0:T(8,128)(2,1)} %bitcast.9), calls=%async_computation.2 | async-start | bytes 4194304 | tf_op jit(solution)/shard_map/all_to_all | solution.py:296
  207.0 25.1 %all-to-all-done.2 = bf16[32,2,128,128]{3,2,1,0:T(8,128)(2,1)} async-done(((bf16[32,2,128,128]{3,2,1,0:T(8,128)(2,1)}), bf16[32,2,128,128]{3,2,1,0:T(8,128)(2,1)}, u32[]{:S(2)}, u32[]{:S(2)}) %all-to-all-start.2) | async-done | bytes 2097184 | tf_op jit(solution)/shard_map/all_to_all | solution.py:296
  232.1 3.2 %gather_fusion.3 = bf16[26,128,128]{2,1,0:T(8,128)(2,1)} fusion(bf16[64,128,128]{2,1,0:T(8,128)(2,1)} %bitcast.10, s32[1024]{0:T(1024)S(1)} %pad_clamp_fusion), kind=kCustom, calls=%fused_computation.3 | custom fusion | bytes 1704040 | tf_op jit(solution)/shard_map/jit(_take)/gather | solution.py:299
  (85 shorter events, 12.8 us)
Async XLA Ops:
  3.8 16.3 %all-to-all-start = ((s32[32,1,2]{2,1,0:T(1,128)}), s32[32,1,2]{2,1,0:T(1,128)S(1)}, u32[]{:S(2)}, u32[]{:S(2)}) async-start(s32[32,1,2]{2,1,0:T(1,128)} %bitcast), calls=%async_computation | async-start | bytes 32768 | tf_op jit(solution)/shard_map/all_to_all | solution.py:226
  25.3 38.7 %copy-start.18 = (s32[4]{0:T(128)S(1)}, s32[4]{0:T(128)}, u32[]{:S(2)}) copy-start(s32[4]{0:T(128)} %constant.74.clone) | copy-start | bytes 52
  25.3 38.8 %copy-start.3 = (bf16[512,1024]{1,0:T(8,128)(2,1)S(1)}, bf16[512,1024]{1,0:T(8,128)(2,1)}, u32[]{:S(2)}) copy-start(bf16[512,1024]{1,0:T(8,128)(2,1)} %param.11) | copy-start | bytes 3145732
  25.3 32.8 %all-to-all-start.1 = ((bf16[32,2,128,128]{3,2,1,0:T(8,128)(2,1)}), bf16[32,2,128,128]{3,2,1,0:T(8,128)(2,1)S(1)}, u32[]{:S(2)}, u32[]{:S(2)}) async-start(bf16[32,2,128,128]{3,2,1,0:T(8,128)(2,1)} %bitcast.20), calls=%async_computation.1 | async-start | bytes 4194304 | tf_op jit(solution)/shard_map/all_to_all | solution.py:236
  58.1 5.9 %copy-start.1 = (bf16[32,2,128,128]{3,2,1,0:T(8,128)(2,1)}, bf16[32,2,128,128]{3,2,1,0:T(8,128)(2,1)S(1)}, u32[]{:S(2)}) copy-start(bf16[32,2,128,128]{3,2,1,0:T(8,128)(2,1)S(1)} %all-to-all-done.1) | copy-start | bytes 6291460
  59.6 14.2 %collective-permute-start = (bf16[2048,128]{1,0:T(8,128)(2,1)}, bf16[2048,128]{1,0:T(8,128)(2,1)}, u32[]{:S(2)}, u32[]{:S(2)}) collective-permute-start(bf16[2048,128]{1,0:T(8,128)(2,1)} %bitcast.32), channel_id=1, source_target_pairs={{0,1},{1,2},{2,3},{3,0},{4,5},{5,6},{6,7},{7,4},{8,9},{9,10},{10,1... | collective-permute-start | bytes 1572872 | tf_op jit(solution)/shard_map/ppermute | solution.py:246
  60.9 12.9 %collective-permute-start.1 = (bf16[2048,128]{1,0:T(8,128)(2,1)}, bf16[2048,128]{1,0:T(8,128)(2,1)}, u32[]{:S(2)}, u32[]{:S(2)}) collective-permute-start(bf16[2048,128]{1,0:T(8,128)(2,1)} %bitcast.33), channel_id=1, source_target_pairs={{0,3},{1,0},{2,1},{3,2},{4,7},{5,4},{6,5},{7,6},{8,11},{9,8},{10,9... | collective-permute-start | bytes 1572872 | tf_op jit(solution)/shard_map/ppermute | solution.py:246
  62.3 23.8 %collective-permute-start.2 = (bf16[2048,128]{1,0:T(8,128)(2,1)}, bf16[2048,128]{1,0:T(8,128)(2,1)}, u32[]{:S(2)}, u32[]{:S(2)}) collective-permute-start(bf16[2048,128]{1,0:T(8,128)(2,1)} %bitcast.34), channel_id=1, source_target_pairs={{0,2},{1,3},{2,0},{3,1},{4,6},{5,7},{6,4},{7,5},{8,10},{9,11},{10,... | collective-permute-start | bytes 1572872 | tf_op jit(solution)/shard_map/ppermute | solution.py:246
  64.0 1.5 copy-start.14
  69.7 50.1 %copy-start.9 = (bf16[16,128,128]{2,1,0:T(8,128)(2,1)}, bf16[16,128,128]{2,1,0:T(8,128)(2,1)S(1)}, u32[]{:S(2)}) copy-start(bf16[16,128,128]{2,1,0:T(8,128)(2,1)S(1)} %gather_fusion.2) | copy-start | bytes 1572868
  86.2 33.7 %collective-permute-start.3 = (bf16[2048,128]{1,0:T(8,128)(2,1)S(1)}, bf16[2048,128]{1,0:T(8,128)(2,1)S(1)}, u32[]{:S(2)}, u32[]{:S(2)}) collective-permute-start(bf16[2048,128]{1,0:T(8,128)(2,1)S(1)} %bitcast.28), channel_id=1, source_target_pairs={{0,1},{1,2},{2,3},{3,0},{4,5},{5,6},{6,7},{7,4},{8,9},{9,10},{10,1... | collective-permute-start | bytes 1572872 | tf_op jit(solution)/shard_map/ppermute | solution.py:246
  86.7 33.1 %collective-permute-start.4 = (bf16[2048,128]{1,0:T(8,128)(2,1)S(1)}, bf16[2048,128]{1,0:T(8,128)(2,1)S(1)}, u32[]{:S(2)}, u32[]{:S(2)}) collective-permute-start(bf16[2048,128]{1,0:T(8,128)(2,1)S(1)} %bitcast.29), channel_id=1, source_target_pairs={{0,3},{1,0},{2,1},{3,2},{4,7},{5,4},{6,5},{7,6},{8,11},{9,8},{10,9... | collective-permute-start | bytes 1572872 | tf_op jit(solution)/shard_map/ppermute | solution.py:246
  88.9 31.0 %collective-permute-start.5 = (bf16[2048,128]{1,0:T(8,128)(2,1)S(1)}, bf16[2048,128]{1,0:T(8,128)(2,1)S(1)}, u32[]{:S(2)}, u32[]{:S(2)}) collective-permute-start(bf16[2048,128]{1,0:T(8,128)(2,1)S(1)} %bitcast.30), channel_id=1, source_target_pairs={{0,2},{1,3},{2,0},{3,1},{4,6},{5,7},{6,4},{7,5},{8,10},{9,11},{10,... | collective-permute-start | bytes 1572872 | tf_op jit(solution)/shard_map/ppermute | solution.py:246
  119.8 4.6 %copy-start.15 = (bf16[2048,128]{1,0:T(8,128)(2,1)}, bf16[2048,128]{1,0:T(8,128)(2,1)S(1)}, u32[]{:S(2)}) copy-start(bf16[2048,128]{1,0:T(8,128)(2,1)S(1)} %collective-permute-done.3.s1) | copy-start | bytes 1572868
  119.9 4.5 %copy-start.16 = (bf16[2048,128]{1,0:T(8,128)(2,1)}, bf16[2048,128]{1,0:T(8,128)(2,1)S(1)}, u32[]{:S(2)}) copy-start(bf16[2048,128]{1,0:T(8,128)(2,1)S(1)} %collective-permute-done.4.s2) | copy-start | bytes 1572868
  119.9 4.5 %copy-start.17 = (bf16[2048,128]{1,0:T(8,128)(2,1)}, bf16[2048,128]{1,0:T(8,128)(2,1)S(1)}, u32[]{:S(2)}) copy-start(bf16[2048,128]{1,0:T(8,128)(2,1)S(1)} %collective-permute-done.5.s3) | copy-start | bytes 1572868
  119.9 28.5 %collective-permute-start.6 = (bf16[2048,128]{1,0:T(8,128)(2,1)}, bf16[2048,128]{1,0:T(8,128)(2,1)S(1)}, u32[]{:S(2)}, u32[]{:S(2)}) collective-permute-start(bf16[2048,128]{1,0:T(8,128)(2,1)} %get-tuple-element.40), channel_id=1, source_target_pairs={{0,3},{1,0},{2,1},{3,2},{4,7},{5,4},{6,5},{7,6},{8,11},{9,8},{10,9... | collective-permute-start | bytes 1572872 | tf_op jit(solution)/shard_map/ppermute | solution.py:246
  121.7 26.7 %collective-permute-start.7 = (bf16[2048,128]{1,0:T(8,128)(2,1)}, bf16[2048,128]{1,0:T(8,128)(2,1)S(1)}, u32[]{:S(2)}, u32[]{:S(2)}) collective-permute-start(bf16[2048,128]{1,0:T(8,128)(2,1)} %get-tuple-element.41), channel_id=1, source_target_pairs={{0,1},{1,2},{2,3},{3,0},{4,5},{5,6},{6,7},{7,4},{8,9},{9,10},{10,1... | collective-permute-start | bytes 1572872 | tf_op jit(solution)/shard_map/ppermute | solution.py:246
  121.7 26.7 %collective-permute-start.8 = (bf16[2048,128]{1,0:T(8,128)(2,1)}, bf16[2048,128]{1,0:T(8,128)(2,1)}, u32[]{:S(2)}, u32[]{:S(2)}) collective-permute-start(bf16[2048,128]{1,0:T(8,128)(2,1)} %get-tuple-element.42), channel_id=1, source_target_pairs={{0,2},{1,3},{2,0},{3,1},{4,6},{5,7},{6,4},{7,5},{8,10},{9,11},{10,... | collective-permute-start | bytes 1572872 | tf_op jit(solution)/shard_map/ppermute | solution.py:246
  148.4 11.4 %copy-start.2 = (bf16[512,2048]{1,0:T(8,128)(2,1)S(1)}, bf16[512,2048]{1,0:T(8,128)(2,1)}, u32[]{:S(2)}) copy-start(bf16[512,2048]{1,0:T(8,128)(2,1)} %get-tuple-element.52) | copy-start | bytes 6291460
  150.7 9.0 %collective-permute-start.12 = (bf16[16,16,2048]{2,1,0:T(8,128)(2,1)S(1)}, bf16[16,16,2048]{2,1,0:T(8,128)(2,1)}, u32[]{:S(2)}, u32[]{:S(2)}) collective-permute-start(bf16[16,16,2048]{2,1,0:T(8,128)(2,1)S(1)} %dynamic-slice_bitcast_fusion), channel_id=1, source_target_pairs={{0,4},{4,0},{8,12},{12,8},{16,20},{20,16},{24,28},{28,24},{32,36},... | collective-permute-start | bytes 3145736 | tf_op jit(solution)/shard_map/ppermute | solution.py:282
  159.7 10.1 %copy-start.4 = (bf16[2048,128]{1,0:T(8,128)(2,1)S(1)}, bf16[2048,128]{1,0:T(8,128)(2,1)}, u32[]{:S(2)}) copy-start(bf16[2048,128]{1,0:T(8,128)(2,1)} %get-tuple-element.39) | copy-start | bytes 1572868
  159.7 10.1 %copy-start.6 = (bf16[2048,128]{1,0:T(8,128)(2,1)S(1)}, bf16[2048,128]{1,0:T(8,128)(2,1)}, u32[]{:S(2)}) copy-start(bf16[2048,128]{1,0:T(8,128)(2,1)} %copy-done.5) | copy-start | bytes 1572868
  162.4 7.4 %copy-start.8 = (bf16[2048,128]{1,0:T(8,128)(2,1)S(1)}, bf16[2048,128]{1,0:T(8,128)(2,1)}, u32[]{:S(2)}) copy-start(bf16[2048,128]{1,0:T(8,128)(2,1)} %copy-done.7) | copy-start | bytes 1572868
  162.4 30.2 %copy-start = (bf16[2048,128]{1,0:T(8,128)(2,1)S(1)}, bf16[2048,128]{1,0:T(8,128)(2,1)}, u32[]{:S(2)}) copy-start(bf16[2048,128]{1,0:T(8,128)(2,1)} %get-tuple-element.48.a) | copy-start | bytes 1572868
  162.4 32.7 %all-to-all-start.3 = ((bf16[16,16,2048]{2,1,0:T(8,128)(2,1)}), bf16[16,16,2048]{2,1,0:T(8,128)(2,1)S(1)}, u32[]{:S(2)}, u32[]{:S(2)}) async-start(bf16[16,16,2048]{2,1,0:T(8,128)(2,1)} %fusion), calls=%async_computation.3 | async-start | bytes 2097152 | tf_op jit(solution)/shard_map/all_to_all | solution.py:292
  166.4 15.4 %collective-permute-start.10 = (bf16[2048,128]{1,0:T(8,128)(2,1)}, bf16[2048,128]{1,0:T(8,128)(2,1)S(1)}, u32[]{:S(2)}, u32[]{:S(2)}) collective-permute-start(bf16[2048,128]{1,0:T(8,128)(2,1)} %get-tuple-element.50), channel_id=1, source_target_pairs={{0,1},{1,2},{2,3},{3,0},{4,5},{5,6},{6,7},{7,4},{8,9},{9,10},{10,1... | collective-permute-start | bytes 1572872 | tf_op jit(solution)/shard_map/ppermute | solution.py:246
  167.4 23.5 %collective-permute-start.11 = (bf16[2048,128]{1,0:T(8,128)(2,1)}, bf16[2048,128]{1,0:T(8,128)(2,1)S(1)}, u32[]{:S(2)}, u32[]{:S(2)}) collective-permute-start(bf16[2048,128]{1,0:T(8,128)(2,1)} %get-tuple-element.51), channel_id=1, source_target_pairs={{0,2},{1,3},{2,0},{3,1},{4,6},{5,7},{6,4},{7,5},{8,10},{9,11},{10,... | collective-permute-start | bytes 1572872 | tf_op jit(solution)/shard_map/ppermute | solution.py:246
  168.1 24.6 %collective-permute-start.9 = (bf16[2048,128]{1,0:T(8,128)(2,1)}, bf16[2048,128]{1,0:T(8,128)(2,1)S(1)}, u32[]{:S(2)}, u32[]{:S(2)}) collective-permute-start(bf16[2048,128]{1,0:T(8,128)(2,1)} %get-tuple-element.49), channel_id=1, source_target_pairs={{0,3},{1,0},{2,1},{3,2},{4,7},{5,4},{6,5},{7,6},{8,11},{9,8},{10,9... | collective-permute-start | bytes 1572872 | tf_op jit(solution)/shard_map/ppermute | solution.py:246
  195.2 8.7 %copy-start.11 = (bf16[256,1024]{1,0:T(8,128)(2,1)S(1)}, bf16[256,1024]{1,0:T(8,128)(2,1)}, u32[]{:S(2)}) copy-start(bf16[256,1024]{1,0:T(8,128)(2,1)} %get-tuple-element.33) | copy-start | bytes 1572868
  195.2 8.7 %copy-start.13 = (bf16[256,1024]{1,0:T(8,128)(2,1)S(1)}, bf16[256,1024]{1,0:T(8,128)(2,1)}, u32[]{:S(2)}) copy-start(bf16[256,1024]{1,0:T(8,128)(2,1)} %get-tuple-element.34) | copy-start | bytes 1572868
  195.2 36.9 %all-to-all-start.2 = ((bf16[32,2,128,128]{3,2,1,0:T(8,128)(2,1)}), bf16[32,2,128,128]{3,2,1,0:T(8,128)(2,1)}, u32[]{:S(2)}, u32[]{:S(2)}) async-start(bf16[32,2,128,128]{3,2,1,0:T(8,128)(2,1)} %bitcast.9), calls=%async_computation.2 | async-start | bytes 4194304 | tf_op jit(solution)/shard_map/all_to_all | solution.py:296
  (4 other events, 4.3 us)
